TPU v7x, 512 devices: a whole 4x8x8 slice. The times are simulated.
512 devices in a mesh: section: 8 (over y_hi, x), dp: 64 (over y_lo, z, core).
Axes of the slice: x: 4, y: 8 (y_hi: 2, y_lo: 4; y = y_hi * 4 + y_lo), z: 8, core: 2. Of those that a mesh axis runs over, the one named last changes fastest.
Arguments:
- embeds: bfloat16 [12288, 3584], P('dp'), may hold values from -16 to 16
- cotangent: bfloat16 [12288, 3584], P('dp'), may hold values from -1 to 1
- adapter_a: bfloat16 [8, 7168, 128], P('section', 'dp'), may hold values from -0.0625 to 0.0625
- adapter_b: bfloat16 [8, 128, 3584], P('section', None, 'dp'), may hold values from -0.5 to 0.5
- norm_gains: float32 [2, 7168], replicated, may hold values from 0.5 to 1.5
Outputs:
- grad_a: float32 [8, 7168, 128], P('section', 'dp')
- grad_b: float32 [8, 128, 3584], P('section')
- grad_gain: float32 [2, 7168], P(None, 'dp')
- grad_embed: bfloat16 [12288, 3584], P('dp', 'section')
All inputs are finite; a program needn't handle non-finite values.
Results may differ from a plain program's by a relative error of at most 0.023.
Values may be sent and summed in bfloat16 or wider, within the bound.
A program may use at most 64 MiB of HBM per device.

v0:
```python
import jax
import jax.numpy as jnp
from jax import lax
from jax.sharding import PartitionSpec as P

MROWS = 24
epsilon = 1e-05


def from_behind(block, axis, distance):
    devices = range(lax.axis_size(axis))
    route = [(i - distance, i) for i in devices if i - distance in devices]
    return lax.ppermute(block, axis, route)


def normalize(hidden, embeds, gain_row):
    joined = jnp.concatenate([hidden.astype(jnp.float32), embeds.astype(jnp.float32)], axis=1)
    inv_rms = lax.rsqrt(jnp.mean(joined * joined, axis=1, keepdims=True) + epsilon)
    normed = joined * inv_rms
    lowered = (normed * gain_row[None, :]).astype(jnp.bfloat16)
    return (normed, inv_rms, lowered)


def contract(left_op, right_op, left_dim, right_dim):
    return lax.dot_general(
        left_op,
        right_op,
        (((left_dim,), (right_dim,)), ((), ())),
        preferred_element_type=jnp.float32,
    )


def pass_on(payload, offset):
    return from_behind(payload, "section", offset)


def pick(stacked, index):
    return lax.dynamic_index_in_dim(stacked, index, 0, keepdims=False)


def place(stacked, index, value, active):
    current = pick(stacked, index)
    return lax.dynamic_update_index_in_dim(stacked, jnp.where(active, value, current), index, 0)


def per_device(embeds, cotangent, adapter_a, adapter_b, norm_gains):
    sections = lax.axis_size("section")
    section_id = lax.axis_index("section")
    down_mat, up_mat = (
        lax.all_gather(adapter_a[0], "dp", axis=0, tiled=True),
        lax.all_gather(adapter_b[0], "dp", axis=1, tiled=True),
    )
    parity = section_id % 2
    gain_row = jnp.where(parity == 0, norm_gains[0], norm_gains[1])
    model_width = embeds.shape[1]
    joined_width = down_mat.shape[0]
    low_rank = down_mat.shape[1]
    group_size = 1
    block_rows = MROWS * group_size
    block_count = embeds.shape[0] // block_rows
    tick_count = block_count + sections - 1
    embed_blocks = embeds.reshape(block_count, block_rows, model_width)
    target_blocks = cotangent.reshape(block_count, block_rows, model_width)

    def forward_tick(tick, state_in):
        incoming, hidden_keep, reduced_keep = state_in
        block_index = tick - section_id
        active = (block_index >= 0) & (block_index < block_count)
        safe_index = jnp.clip(block_index, 0, block_count - 1)
        embed_block = pick(embed_blocks, safe_index)
        hidden = jnp.where(section_id == 0, embed_block, incoming)
        normed, inv_rms, lowered = normalize(hidden, embed_block, gain_row)
        reduced = jnp.dot(lowered, down_mat, preferred_element_type=jnp.float32).astype(
            jnp.bfloat16
        )
        output = (
            hidden.astype(jnp.float32)
            + jnp.dot(reduced, up_mat, preferred_element_type=jnp.float32)
        ).astype(jnp.bfloat16)
        hidden_keep = place(hidden_keep, safe_index, hidden, active)
        reduced_keep = place(reduced_keep, safe_index, reduced, active)
        outgoing = jnp.where(active, output, jnp.zeros_like(output))
        return (pass_on(outgoing, 1), hidden_keep, reduced_keep)

    forward_init = (
        jnp.zeros((block_rows, model_width), jnp.bfloat16),
        jnp.zeros((block_count, block_rows, model_width), jnp.bfloat16),
        jnp.zeros((block_count, block_rows, low_rank), jnp.bfloat16),
    )
    last_sent, hidden_keep, reduced_keep = lax.fori_loop(0, tick_count, forward_tick, forward_init)

    def backward_tick(tick, state_in):
        incoming, grad_a, grad_b, gain_acc, term_keep = state_in
        block_index = tick - (sections - 1 - section_id)
        active = (block_index >= 0) & (block_index < block_count)
        safe_index = jnp.clip(block_index, 0, block_count - 1)
        target = pick(target_blocks, safe_index)
        back_in = jnp.where(section_id == sections - 1, target, incoming)
        back_in = jnp.where(active, back_in, jnp.zeros_like(back_in))
        hidden = pick(hidden_keep, safe_index)
        reduced = pick(reduced_keep, safe_index)
        embed_block = pick(embed_blocks, safe_index)
        normed, inv_rms, lowered = normalize(hidden, embed_block, gain_row)
        up_grad = contract(back_in, up_mat, 1, 1).astype(jnp.bfloat16)
        grad_b = grad_b + contract(reduced, back_in, 0, 0)
        grad_lowered = contract(up_grad, down_mat, 1, 1)
        grad_a = grad_a + contract(lowered, up_grad, 0, 0)
        gain_acc = gain_acc + jnp.sum(grad_lowered * normed, axis=0)
        scaled = grad_lowered * gain_row[None, :]
        grad_joined = inv_rms * (scaled - normed * jnp.mean(scaled * normed, axis=1, keepdims=True))
        back_out = (back_in.astype(jnp.float32) + grad_joined[:, :model_width]).astype(jnp.bfloat16)
        embed_tail = grad_joined[:, model_width:] + jnp.where(
            section_id == 0, back_out.astype(jnp.float32), 0.0
        )
        term_keep = place(term_keep, safe_index, embed_tail.astype(jnp.bfloat16), active)
        return (pass_on(back_out, -1), grad_a, grad_b, gain_acc, term_keep)

    backward_init = (
        jnp.zeros((block_rows, model_width), jnp.bfloat16),
        jnp.zeros((joined_width, low_rank), jnp.float32),
        jnp.zeros((low_rank, model_width), jnp.float32),
        jnp.zeros((joined_width,), jnp.float32),
        jnp.zeros((block_count, block_rows, model_width), jnp.bfloat16),
    )
    last_back, grad_a, grad_b, gain_acc, term_keep = lax.fori_loop(
        0, tick_count, backward_tick, backward_init
    )
    gain_pair = jnp.stack(
        [jnp.where(parity == 0, gain_acc, 0.0), jnp.where(parity == 1, gain_acc, 0.0)]
    )
    grad_a_part, gain_part = (
        lax.psum_scatter(grad_a, "dp", scatter_dimension=0, tiled=True),
        lax.psum_scatter(gain_pair, "dp", scatter_dimension=1, tiled=True),
    )
    grad_b_sum = lax.psum(grad_b, "dp")
    embed_terms = term_keep.reshape(-1, model_width).astype(jnp.float32)
    embed_sum, gain_sum = (
        lax.psum(embed_terms.astype(jnp.bfloat16), "section").astype(jnp.float32),
        lax.psum(gain_part.astype(jnp.bfloat16), "section").astype(jnp.float32),
    )
    column_count = model_width // sections
    embed_cols = lax.dynamic_slice_in_dim(embed_sum, section_id * column_count, column_count, 1)
    return (grad_a_part[None], grad_b_sum[None], gain_sum, embed_cols.astype(jnp.bfloat16))


def solution(mesh):
    in_specs = (
        P("dp", None),
        P("dp", None),
        P("section", "dp", None),
        P("section", None, "dp"),
        P(),
    )
    out_specs = (
        P("section", "dp", None),
        P("section", None, None),
        P(None, "dp"),
        P("dp", "section"),
    )
    return jax.shard_map(
        per_device, mesh=mesh, in_specs=in_specs, out_specs=out_specs, check_vma=False
    )
```

profile of v0, /device:TPU:2, one launch (start us, length us, event | category | flops | bytes accessed | tf_op | source)
XLA Modules:
  0.0 1952.0 jit_solution(14938094379765959038)
XLA Ops:
  8.0 88.9 %all-gather.1 = bf16[1,128,3584]{1,2,0:T(8,128)(2,1)S(1)} all-gather(bf16[1,128,56]{1,2,0:T(8,128)(2,1)} %param.12), channel_id=3, replica_groups=mesh['section'=8,'dp'=64] {'dp'}, dimensions={2}, use_global_device_ids=true | all-gather | bytes 931840 | tf_op jit(solution)/shard_map/all_gather | solution.py:51
  97.4 34.4 %all-gather.4.cloned.1.call-done = bf16[1,7168,128]{2,1,0:T(8,128)(2,1)} async-done(((bf16[1,112,128]{2,1,0:T(8,128)(2,1)}), bf16[1,7168,128]{2,1,0:T(8,128)(2,1)}) %all-gather.4.cloned.1.call-update) | async-done | bytes 1835024 | tf_op jit(solution)/shard_map/all_gather | solution.py:50
  133.7 259.5 %while.42 = (s32[]{:T(128)}, bf16[24,3584]{1,0:T(8,128)(2,1)S(1)}, bf16[8,24,3584]{2,1,0:T(8,128)(2,1)}, bf16[8,24,128]{2,1,0:T(8,128)(2,1)}, s32[]{:T(128)}, /*...) while((s32[]{:T(128)}, bf16[24,3584]{1,0:T(8,128)(2,1)S(1)}, ...), condition=%wide.region_2.3_spmd, body=%wide.region_0.2_spmd.sunk | while | flops 67958816 | bytes 14632085 | solution.py:90
  177.5 10.4 collective-permute-start
  195.8 10.5 collective-permute-start
  214.2 10.4 collective-permute-start
  232.5 10.4 collective-permute-start
  250.8 10.5 collective-permute-start
  269.2 10.5 collective-permute-start
  287.6 10.5 collective-permute-start
  306.0 10.5 collective-permute-start
  324.4 10.5 collective-permute-start
  342.8 10.5 collective-permute-start
  361.2 10.5 collective-permute-start
  379.5 10.8 collective-permute-start
  395.1 308.1 %while.43 = (s32[]{:T(128)}, bf16[24,3584]{1,0:T(8,128)(2,1)}, f32[7168,128]{1,0:T(8,128)}, f32[128,3584]{1,0:T(8,128)}, f32[7168]{0:T(1024)S(1)}, /*index=5*/bf...) while((s32[]{:T(128)}, bf16[24,3584]{1,0:T(8,128)(2,1)}, ...), condition=%wide.region_7.8_spmd.clone, body=%wide.region_3.7_spmd.clone.sunk | while | flops 141248544 | bytes 44095332 | solution.py:125
  406.9 8.3 collective-permute-done.1
  429.9 6.7 collective-permute-done.1
  451.3 8.7 collective-permute-done.1
  707.7 296.9 %reduce-scatter.7.cloned.1.call-done = f32[112,2]{1,0:T(8,128)} async-done(((f32[7168,2]{1,0:T(8,128)}), f32[112,2]{1,0:T(8,128)}) %reduce-scatter.7.cloned.1.call-update) | async-done | bytes 912
  1005.5 24.4 %psum.22 = bf16[2,112]{1,0:T(2,128)(2,1)S(1)} all-reduce(bf16[2,112]{1,0:T(2,128)(2,1)S(1)} %copy.13), channel_id=1, replica_groups=mesh['section'=8,'dp'=64] {'section'}, use_global_device_ids=true, to_apply=%region_11.12 | all-reduce | flops 224 | bytes 896 | tf_op jit(solution)/shard_map/psum | solution.py:139
  1030.4 90.8 %all-reduce.5.cloned.1.call-done = bf16[192,3584]{1,0:T(8,128)(2,1)} async-done(((bf16[192,3584]{1,0:T(8,128)(2,1)}), bf16[192,3584]{1,0:T(8,128)(2,1)}) %all-reduce.5.cloned.1.call-update) | async-done | bytes 1376272 | tf_op jit(solution)/shard_map/psum | solution.py:138
  1123.0 533.6 %all-reduce.3.cloned.1.call-done = f32[1,128,3584]{2,1,0:T(8,128)} async-done(((f32[1,128,3584]{2,1,0:T(8,128)}), f32[1,128,3584]{2,1,0:T(8,128)}) %all-reduce.3.cloned.1.call-update) | async-done | bytes 1835024 | tf_op jit(solution)/shard_map/psum | solution.py:135
  1656.6 286.1 %reduce-scatter.5.cloned.1.call-done = f32[112,128]{1,0:T(8,128)} async-done(((f32[7168,128]{1,0:T(8,128)}), f32[112,128]{1,0:T(8,128)}) %reduce-scatter.5.cloned.1.call-update) | async-done | bytes 57360 | tf_op jit(solution)/shard_map/reduce_scatter | solution.py:132
  (539 shorter events, 431.7 us)
Async XLA Ops:
  7.2 124.7 %all-gather.4.cloned.1.call-start = ((), (), s32[]{:S(2)}) async-start(), calls=%async_computation.5 | async-start | bytes 1863680 | tf_op jit(solution)/shard_map/all_gather | solution.py:50
  7.9 996.7 %reduce-scatter.7.cloned.1.call-start = ((), (), s32[]{:S(2)}) async-start(), calls=%async_computation.6 | async-start | bytes 3727360
  195.8 13.4 collective-permute-start
  250.8 13.4 collective-permute-start
  287.6 13.4 collective-permute-start
  306.0 13.4 collective-permute-start
  361.2 13.4 collective-permute-start
  379.5 13.7 collective-permute-start
  401.0 14.2 collective-permute-start.1
  421.9 14.8 collective-permute-start.1
  443.3 16.8 collective-permute-start.1
  466.6 14.4 collective-permute-start.1
  527.1 13.6 collective-permute-start.1
  547.3 13.6 collective-permute-start.1
  567.5 13.6 collective-permute-start.1
  587.8 13.6 collective-permute-start.1
  608.0 13.6 collective-permute-start.1
  628.2 13.6 collective-permute-start.1
  648.5 13.6 collective-permute-start.1
  668.7 13.6 collective-permute-start.1
  688.9 13.6 collective-permute-start.1
  705.8 415.5 %all-reduce.5.cloned.1.call-start = ((), (), s32[]{:S(2)}) async-start(), calls=%async_computation.4 | async-start | bytes 2752512 | tf_op jit(solution)/shard_map/psum | solution.py:138
  706.5 950.1 %all-reduce.3.cloned.1.call-start = ((), (), s32[]{:S(2)}) async-start(), calls=%async_computation.3 | async-start | bytes 3670016 | tf_op jit(solution)/shard_map/psum | solution.py:135
  707.1 1235.6 %reduce-scatter.5.cloned.1.call-start = ((), (), s32[]{:S(2)}) async-start(), calls=%async_computation.2 | async-start | bytes 3727360 | tf_op jit(solution)/shard_map/reduce_scatter | solution.py:132
  (87 other events, 501.0 us)
Sparse Core Ops, SparseCore 0:
  10.2 121.6 all-gather.3
  705.9 298.6 reduce-scatter.6
  1007.8 113.3 all-reduce.4
  1124.6 531.9 all-reduce.2
  1660.0 282.5 reduce-scatter.4
where the time goes:
time: 1960 us; the launch traced here: 1950 us
  waiting for transfers between devices  1380 us (70%)
  starting transfers between devices  167 us (9%)
  matrix products  132 us (7%)
  blocking collectives  113 us (6%)
  local copies, waits for them, and re-layouts  78.5 us (4%)
  other arithmetic  64.9 us (3%)
    psum x1, waiting for transfers between devices, per_device(): grad_b_sum = lax.psum(grad_b, 'dp')  534 us
    unnamed x6, waiting for transfers between devices  299 us
    reduce_scatter x1, waiting for transfers between devices, per_device(): lax.psum_scatter(grad_a, 'dp', scatter_dimension=0, tiled=True)  286 us
    ppermute x30, starting transfers between devices, from_behind(): return lax.ppermute(block, axis, route)  166 us
    ppermute x30, waiting for transfers between devices, from_behind(): return lax.ppermute(block, axis, route)  137 us
    dot_general x60, matrix products, contract(): lax.dot_general(left_op, right_op, (((left_dim,), (right_dim,)), ((), ())...  112 us
    psum x1, waiting for transfers between devices, per_device(): lax.psum(embed_terms.astype(jnp.bfloat16), 'section').astype(jnp.float32)  90.8 us
    all_gather x1, blocking collectives, per_device(): lax.all_gather(adapter_b[0], 'dp', axis=1, tiled=True)  88.9 us
  transfers between devices with their start and end apart: 35, of which 35 were waited for; matrix products, arithmetic and copies ran while one was open for 5% of the time, Pallas kernels for 0%

commit v1 on v0

--- a/solution.py
+++ b/solution.py
@@ -5,6 +5,11 @@
 
 MROWS = 24
 epsilon = 1e-05
+
+
+def gather_and_add(block, name):
+    parts = lax.all_gather(block, name)
+    return jnp.sum(parts, axis=0)
 
 
 def from_behind(block, axis, distance):
@@ -135,7 +140,7 @@
     grad_b_sum = lax.psum(grad_b, "dp")
     embed_terms = term_keep.reshape(-1, model_width).astype(jnp.float32)
     embed_sum, gain_sum = (
-        lax.psum(embed_terms.astype(jnp.bfloat16), "section").astype(jnp.float32),
+        gather_and_add(embed_terms.astype(jnp.bfloat16), "section").astype(jnp.float32),
         lax.psum(gain_part.astype(jnp.bfloat16), "section").astype(jnp.float32),
     )
     column_count = model_width // sections

time: 1960 us -> 2040 us (1.041)
  waiting for transfers between devices: 1380 us -> 1470 us
    all_gather x0 -> x1, waiting for transfers between devices: none -> 190 us  [gather_and_add(): parts = lax.all_gather(block, name)]
    psum x1 -> x0, waiting for transfers between devices: 90.8 us -> none  [per_device(): lax.psum(embed_terms.astype(jnp.bfloat16), 'section').astype(jnp.float32)]
where the time goes in v1:
time: 2040 us
  waiting for transfers between devices  1470 us (72%)
  starting transfers between devices  167 us (8%)
  matrix products  133 us (7%)
  blocking collectives  112 us (5%)
  other arithmetic  69.2 us (3%)
  local copies, waits for them, and re-layouts  67.9 us (3%)
    psum x1, waiting for transfers between devices, per_device(): grad_b_sum = lax.psum(grad_b, 'dp')  523 us
    unnamed x6, waiting for transfers between devices  302 us
    reduce_scatter x1, waiting for transfers between devices, per_device(): lax.psum_scatter(grad_a, 'dp', scatter_dimension=0, tiled=True)  286 us
    all_gather x1, waiting for transfers between devices, gather_and_add(): parts = lax.all_gather(block, name)  190 us
    ppermute x30, starting transfers between devices, from_behind(): return lax.ppermute(block, axis, route)  166 us
    ppermute x30, waiting for transfers between devices, from_behind(): return lax.ppermute(block, axis, route)  135 us
    dot_general x60, matrix products, contract(): lax.dot_general(left_op, right_op, (((left_dim,), (right_dim,)), ((), ())...  114 us
    all_gather x1, blocking collectives, per_device(): lax.all_gather(adapter_b[0], 'dp', axis=1, tiled=True)  88.8 us
  transfers between devices with their start and end apart: 35, of which 35 were waited for; matrix products, arithmetic and copies ran while one was open for 5% of the time, Pallas kernels for 0%

profile of v1, /device:TPU:2, one launch (start us, length us, event | category | flops | bytes accessed | tf_op | source)
XLA Modules:
  0.0 2035.9 jit_solution(14215943740278383939)
XLA Ops:
  8.0 88.8 %all-gather.1 = bf16[1,128,3584]{1,2,0:T(8,128)(2,1)S(1)} all-gather(bf16[1,128,56]{1,2,0:T(8,128)(2,1)} %param.12), channel_id=3, replica_groups=mesh['section'=8,'dp'=64] {'dp'}, dimensions={2}, use_global_device_ids=true | all-gather | bytes 931840 | tf_op jit(solution)/shard_map/all_gather | solution.py:56
  97.4 34.4 %all-gather.7.cloned.1.call-done = bf16[1,7168,128]{2,1,0:T(8,128)(2,1)} async-done(((bf16[1,112,128]{2,1,0:T(8,128)(2,1)}), bf16[1,7168,128]{2,1,0:T(8,128)(2,1)}) %all-gather.7.cloned.1.call-update) | async-done | bytes 1835024 | tf_op jit(solution)/shard_map/all_gather | solution.py:55
  133.7 259.4 %while.42 = (s32[]{:T(128)}, bf16[24,3584]{1,0:T(8,128)(2,1)S(1)}, bf16[8,24,3584]{2,1,0:T(8,128)(2,1)}, bf16[8,24,128]{2,1,0:T(8,128)(2,1)}, s32[]{:T(128)}, /*...) while((s32[]{:T(128)}, bf16[24,3584]{1,0:T(8,128)(2,1)S(1)}, ...), condition=%wide.region_2.3_spmd, body=%wide.region_0.2_spmd.sunk | while | flops 67958816 | bytes 14632085 | solution.py:95
  177.5 10.4 collective-permute-start
  195.8 10.5 collective-permute-start
  214.1 10.4 collective-permute-start
  232.4 10.4 collective-permute-start
  250.7 10.5 collective-permute-start
  269.1 10.5 collective-permute-start
  287.5 10.5 collective-permute-start
  305.9 10.5 collective-permute-start
  324.2 10.5 collective-permute-start
  342.6 10.5 collective-permute-start
  361.0 10.5 collective-permute-start
  379.4 10.8 collective-permute-start
  394.3 296.4 %while.43 = (s32[]{:T(128)}, bf16[24,3584]{1,0:T(8,128)(2,1)S(1)}, f32[7168,128]{1,0:T(8,128)}, f32[128,3584]{1,0:T(8,128)}, f32[7168]{0:T(1024)S(1)}, /*index=5...) while((s32[]{:T(128)}, bf16[24,3584]{1,0:T(8,128)(2,1)S(1)}, ...), condition=%wide.region_7.8_spmd.clone, body=%wide.region_3.7_spmd.clone.sunk | while | flops 141248544 | bytes 43407176 | solution.py:130
  406.1 8.5 collective-permute-done.1
  428.7 7.7 collective-permute-done.1
  450.4 7.4 collective-permute-done.1
  695.1 299.6 %reduce-scatter.7.cloned.1.call-done = f32[112,2]{1,0:T(8,128)} async-done(((f32[7168,2]{1,0:T(8,128)}), f32[112,2]{1,0:T(8,128)}) %reduce-scatter.7.cloned.1.call-update) | async-done | bytes 912
  995.6 23.6 %psum.15 = bf16[2,112]{1,0:T(2,128)(2,1)S(1)} all-reduce(bf16[2,112]{1,0:T(2,128)(2,1)S(1)} %copy.13), channel_id=1, replica_groups=mesh['section'=8,'dp'=64] {'section'}, use_global_device_ids=true, to_apply=%region_11.12 | all-reduce | flops 224 | bytes 896 | tf_op jit(solution)/shard_map/psum | solution.py:144
  1019.9 190.4 %all-gather.5.cloned.1.call-done = bf16[8,192,3584]{2,1,0:T(8,128)(2,1)} async-done(((bf16[1,192,3584]{2,1,0:T(8,128)(2,1)}), bf16[8,192,3584]{2,1,0:T(8,128)(2,1)}) %all-gather.5.cloned.1.call-update) | async-done | bytes 11010064 | tf_op jit(solution)/shard_map/all_gather | solution.py:11
  1217.5 523.2 %all-reduce.2.cloned.1.call-done = f32[1,128,3584]{2,1,0:T(8,128)} async-done(((f32[1,128,3584]{2,1,0:T(8,128)}), f32[1,128,3584]{2,1,0:T(8,128)}) %all-reduce.2.cloned.1.call-update) | async-done | bytes 1835024 | tf_op jit(solution)/shard_map/psum | solution.py:140
  1740.7 285.8 %reduce-scatter.5.cloned.1.call-done = f32[112,128]{1,0:T(8,128)} async-done(((f32[7168,128]{1,0:T(8,128)}), f32[112,128]{1,0:T(8,128)}) %reduce-scatter.5.cloned.1.call-update) | async-done | bytes 57360 | tf_op jit(solution)/shard_map/reduce_scatter | solution.py:137
  (510 shorter events, 424.9 us)
Async XLA Ops:
  7.2 124.7 %all-gather.7.cloned.1.call-start = ((), (), s32[]{:S(2)}) async-start(), calls=%async_computation.5 | async-start | bytes 1863680 | tf_op jit(solution)/shard_map/all_gather | solution.py:55
  7.9 986.9 %reduce-scatter.7.cloned.1.call-start = ((), (), s32[]{:S(2)}) async-start(), calls=%async_computation.6 | async-start | bytes 3727360
  195.8 13.4 collective-permute-start
  250.7 13.4 collective-permute-start
  287.5 13.4 collective-permute-start
  324.2 13.4 collective-permute-start
  342.6 13.4 collective-permute-start
  379.4 13.7 collective-permute-start
  400.2 14.5 collective-permute-start.1
  420.6 15.8 collective-permute-start.1
  442.3 15.6 collective-permute-start.1
  501.6 13.6 collective-permute-start.1
  521.1 13.6 collective-permute-start.1
  540.6 13.6 collective-permute-start.1
  560.0 13.6 collective-permute-start.1
  579.6 13.6 collective-permute-start.1
  599.0 13.6 collective-permute-start.1
  618.5 13.6 collective-permute-start.1
  638.0 13.7 collective-permute-start.1
  657.6 13.6 collective-permute-start.1
  677.1 13.6 collective-permute-start.1
  693.2 517.0 %all-gather.5.cloned.1.call-start = ((), (), s32[]{:S(2)}) async-start(), calls=%async_computation.4 | async-start | bytes 12386304 | tf_op jit(solution)/shard_map/all_gather | solution.py:11
  694.0 1046.7 %all-reduce.2.cloned.1.call-start = ((), (), s32[]{:S(2)}) async-start(), calls=%async_computation.3 | async-start | bytes 3670016 | tf_op jit(solution)/shard_map/psum | solution.py:140
  694.5 1332.0 %reduce-scatter.5.cloned.1.call-start = ((), (), s32[]{:S(2)}) async-start(), calls=%async_computation.2 | async-start | bytes 3727360 | tf_op jit(solution)/shard_map/reduce_scatter | solution.py:137
  (72 other events, 475.2 us)
Sparse Core Ops, SparseCore 0:
  10.2 121.6 all-gather.6
  693.3 301.3 reduce-scatter.6
  998.4 211.7 all-gather.4
  1213.9 526.7 all-reduce.1
  1743.9 282.5 reduce-scatter.4
